TPU v7x, 32 devices: a whole 2x2x4 slice. The times are simulated.
32 devices in a mesh: seq: 8 (over y, x, core), dp: 4 (over z).
Axes of the slice: x: 2, y: 2, z: 4, core: 2. Of those that a mesh axis runs over, the one named last changes fastest.
Arguments:
- inputs: bfloat16 [2, 64, 512, 512], P(None, 'seq', 'dp'), may hold values from -6 to 6
- cotangent: bfloat16 [2, 64, 512, 512], P(None, 'seq', 'dp'), may hold values from -6 to 6
- lengths: int32 [2, 64], P(None, 'seq'), may hold values from 64 to 512, as said below
- weights: float32 [48, 256, 256], P('dp', 'seq'), may hold values from -0.3005204 to 0.3005204
- vectors: float32 [6144], replicated, may hold values from -0.35 to 1.3
- positions: float32 [512, 512], P('dp'), may hold values from -3 to 3
- left_stats: float32 [48, 256, 256], P('dp', 'seq'), may hold values from -4.8828125e-05 to 0.00390625
- right_stats: float32 [48, 256, 256], P('dp', 'seq'), may hold values from -4.8828125e-05 to 0.00390625
- left_roots: float32 [48, 256, 256], P('dp', 'seq'), may hold values from -1.13137085 to 11.313708
- right_roots: float32 [48, 256, 256], P('dp', 'seq'), may hold values from -1.13137085 to 11.313708
- vector_second: float32 [6144], replicated, may hold values from 3.8146973e-06 to 1.5258789e-05
- position_second: float32 [512, 512], P('dp'), may hold values from 7.450581e-09 to 2.9802322e-08
Outputs:
- layer_out: bfloat16 [2, 64, 512, 512], P(None, 'seq', 'dp')
- input_grad: float32 [2, 64, 512, 512], P(None, 'seq', 'dp')
- block_grads: float32 [48, 256, 256], P('dp', 'seq')
- left_new: float32 [48, 256, 256], P('dp', 'seq')
- right_new: float32 [48, 256, 256], P('dp', 'seq')
- weights_new: float32 [48, 256, 256], P('dp', 'seq')
- vector_grads: float32 [6144], replicated
- vector_second_new: float32 [6144], replicated
- vectors_new: float32 [6144], replicated
- position_grads: float32 [512, 512], P('dp')
- position_second_new: float32 [512, 512], P('dp')
- positions_new: float32 [512, 512], P('dp')
Inputs may be any that keep to these rules, and one draw needn't show every extreme that they name: `lengths`: for every index of seq, one of its 2 x 8 windows holds exactly 512 valid characters.
All inputs are finite; a program needn't handle non-finite values.
Results may differ from a plain program's by a relative error of at most 0.02.
The roundings to bfloat16 on the way count: a program that leaves them out, or rounds other values in their place, can miss the bound.
Values may be sent and summed in bfloat16 or wider, within the bound.
No kernel may reach another device: no remote copies, remote signals or barrier semaphores. Data moves between devices by JAX's collectives and lax.ppermute only.
A program may use at most 256 MiB of HBM per device.

v0:
```python
import jax
import jax.numpy as jnp
from jax import lax
from jax.sharding import PartitionSpec as P

HEADS = 8
FF = 2048


NORM_EPS = 1e-05
ROOT_EPS = 1e-08
DECAY = 0.5
MATRIX_RATE = 0.5
VECTOR_RATE = 0.2
MASKED = -1e30


def layer_norm(values, gain, shift):
    centered = values - jnp.mean(values, axis=-1, keepdims=True)
    spread = jnp.mean(centered * centered, axis=-1, keepdims=True)
    return centered * lax.rsqrt(spread + NORM_EPS) * gain + shift


def gelu_exact(values):
    return jax.nn.gelu(values, approximate=False)


def to_blocks(matrix, block_size):
    rows, cols = matrix.shape
    grid = matrix.reshape(rows // block_size, block_size, cols // block_size, block_size)
    return grid.transpose(0, 2, 1, 3).reshape(-1, block_size, block_size)


def from_blocks(block_stack, rows, cols):
    block_size = block_stack.shape[-1]
    grid = block_stack.reshape(rows // block_size, cols // block_size, block_size, block_size)
    return grid.transpose(0, 2, 1, 3).reshape(rows, cols)


def product_low(left_rows, right_matrix):
    return jnp.dot(left_rows, right_matrix, preferred_element_type=jnp.float32)


def product_back(left_rows, right_matrix):
    return jnp.einsum("re,de->rd", left_rows, right_matrix, preferred_element_type=jnp.float32)


def product_outer(left_rows, right_rows):
    return jnp.einsum("rd,re->de", left_rows, right_rows, preferred_element_type=jnp.float32)


def column_sum(rows):
    return jnp.sum(rows.astype(jnp.float32), axis=0)


def body(
    inputs,
    cotangent,
    lengths,
    weights,
    vectors,
    positions,
    left_stats,
    right_stats,
    left_roots,
    right_roots,
    vector_second,
    position_second,
):
    seq_count = lax.axis_size("seq")
    dp_count = lax.axis_size("dp")
    seq_index = lax.axis_index("seq")
    dp_index = lax.axis_index("dp")
    micro, wins_dev, segment, model_width = inputs.shape
    window = segment * dp_count
    total_tokens = micro * wins_dev * seq_count * window
    hidden = FF
    head_count = HEADS
    head_dim = model_width // head_count
    heads_here = head_count // dp_count
    group_width = heads_here * head_dim
    score_scale = head_dim ** (-0.5)
    owned_blocks, row_part, block_size = weights.shape
    gathered = lax.all_gather(
        weights[None].astype(jnp.bfloat16), ("seq", "dp"), axis=0, tiled=True
    ).astype(jnp.float32)
    gathered = gathered.reshape(seq_count, dp_count, owned_blocks, row_part, block_size)
    block_stack = gathered.transpose(1, 2, 0, 3, 4).reshape(
        dp_count * owned_blocks, block_size, block_size
    )
    square = (model_width // block_size) ** 2
    wide = model_width // block_size * (hidden // block_size)
    w_query = from_blocks(block_stack[0:square], model_width, model_width)
    w_key = from_blocks(block_stack[square : 2 * square], model_width, model_width)
    w_value = from_blocks(block_stack[2 * square : 3 * square], model_width, model_width)
    w_joined = jnp.concatenate([w_query, w_key, w_value], axis=1).reshape(
        model_width, 3, dp_count, group_width
    )
    w_qkv = (
        w_joined.transpose(0, 2, 1, 3).reshape(model_width, 3 * model_width).astype(jnp.bfloat16)
    )
    w_out = from_blocks(block_stack[3 * square : 4 * square], model_width, model_width).astype(
        jnp.bfloat16
    )
    w_up = from_blocks(block_stack[4 * square : 4 * square + wide], model_width, hidden).astype(
        jnp.bfloat16
    )
    w_down = from_blocks(block_stack[4 * square + wide :], hidden, model_width).astype(jnp.bfloat16)
    offset_base = 3 * model_width + hidden
    bias_query = vectors[0:model_width]
    bias_value = vectors[model_width : 2 * model_width]
    bias_out = vectors[2 * model_width : 3 * model_width]
    bias_up = vectors[3 * model_width : offset_base]
    bias_down = vectors[offset_base : offset_base + model_width]
    gain_one = vectors[offset_base + model_width : offset_base + 2 * model_width]
    shift_one = vectors[offset_base + 2 * model_width : offset_base + 3 * model_width]
    gain_two = vectors[offset_base + 3 * model_width : offset_base + 4 * model_width]
    shift_two = vectors[offset_base + 4 * model_width : offset_base + 5 * model_width]
    bias_joined = jnp.stack(
        [bias_query, jnp.zeros((model_width,), jnp.float32), bias_value]
    ).reshape(3, dp_count, group_width)
    bias_qkv = bias_joined.transpose(1, 0, 2).reshape(3 * model_width)
    places = jnp.arange(window, dtype=jnp.int32)
    causal = places[None, :] <= places[:, None]
    local_places = dp_index * segment + jnp.arange(segment, dtype=jnp.int32)
    grad_qkv = jnp.zeros((model_width, 3 * model_width), jnp.float32)
    grad_out = jnp.zeros((model_width, model_width), jnp.float32)
    grad_up = jnp.zeros((model_width, hidden), jnp.float32)
    grad_down = jnp.zeros((hidden, model_width), jnp.float32)
    grad_bias_qkv = jnp.zeros((3 * model_width,), jnp.float32)
    grad_bias_out = jnp.zeros((model_width,), jnp.float32)
    grad_bias_up = jnp.zeros((hidden,), jnp.float32)
    grad_bias_down = jnp.zeros((model_width,), jnp.float32)
    norm_grads = [jnp.zeros((model_width,), jnp.float32) for piece_index in range(4)]
    grad_positions = jnp.zeros((segment, model_width), jnp.float32)
    layer_rows = []
    input_rows = []
    for micro_step in range(micro):
        lens_here = lengths[micro_step]
        allowed = causal[None, None] & (
            places[None, None, None, :] < lens_here[:, None, None, None]
        )
        start_vals = (inputs[micro_step].astype(jnp.float32) + positions[None]).reshape(
            -1, model_width
        )
        start_low = start_vals.astype(jnp.bfloat16)
        qkv_rows = (product_low(start_low, w_qkv) + bias_qkv).astype(jnp.bfloat16)
        windowed = lax.all_to_all(
            qkv_rows.reshape(wins_dev, segment, dp_count, 3 * group_width),
            "dp",
            split_axis=2,
            concat_axis=1,
            tiled=True,
        )
        windowed = windowed.reshape(wins_dev, window, 3 * group_width)
        queries = windowed[:, :, 0:group_width].reshape(wins_dev, window, heads_here, head_dim)
        key_rows = windowed[:, :, group_width : 2 * group_width].reshape(
            wins_dev, window, heads_here, head_dim
        )
        values = windowed[:, :, 2 * group_width :].reshape(wins_dev, window, heads_here, head_dim)
        scores = (
            jnp.einsum("wqhd,wkhd->whqk", queries, key_rows, preferred_element_type=jnp.float32)
            * score_scale
        )
        scores = jnp.where(allowed, scores, MASKED)
        row_top = jnp.max(scores, axis=-1, keepdims=True)
        expo_terms = jnp.exp(scores - row_top)
        row_total = jnp.sum(expo_terms, axis=-1, keepdims=True)
        attn_probs = expo_terms / row_total
        log_total = row_top + jnp.log(row_total)
        attended = jnp.einsum(
            "whqk,wkhd->wqhd",
            attn_probs.astype(jnp.bfloat16),
            values,
            preferred_element_type=jnp.float32,
        )
        attended = attended.astype(jnp.bfloat16).reshape(wins_dev, window, 1, group_width)
        returned = lax.all_to_all(attended, "dp", split_axis=1, concat_axis=2, tiled=True).reshape(
            -1, model_width
        )
        mixed_rows = start_vals + product_low(returned, w_out) + bias_out
        normed, norm_pull = jax.vjp(layer_norm, mixed_rows, gain_one, shift_one)
        normed_low = normed.astype(jnp.bfloat16)
        up_rows = product_low(normed_low, w_up) + bias_up
        activated, gelu_pull = jax.vjp(gelu_exact, up_rows)
        activated_low = activated.astype(jnp.bfloat16)
        summed = normed + product_low(activated_low, w_down) + bias_down
        result, final_pull = jax.vjp(layer_norm, summed, gain_two, shift_two)
        layer_rows.append(result.astype(jnp.bfloat16).reshape(wins_dev, segment, model_width))
        valid = (local_places[None, :] < lens_here[:, None]).astype(jnp.float32)
        seed_grad = (
            cotangent[micro_step].astype(jnp.float32) * valid[:, :, None] / total_tokens
        ).reshape(-1, model_width)
        d_summed, d_gain_two, d_shift_two = final_pull(seed_grad)
        d_branch_ff = d_summed.astype(jnp.bfloat16)
        (d_up,) = gelu_pull(product_back(d_branch_ff, w_down))
        d_up_low = d_up.astype(jnp.bfloat16)
        d_normed = d_summed + product_back(d_up_low, w_up)
        d_mixed, d_gain_one, d_shift_one = norm_pull(d_normed)
        d_branch_attn = d_mixed.astype(jnp.bfloat16)
        d_returned = product_back(d_branch_attn, w_out).astype(jnp.bfloat16)
        d_windowed = lax.all_to_all(
            d_returned.reshape(wins_dev, segment, dp_count, group_width),
            "dp",
            split_axis=2,
            concat_axis=1,
            tiled=True,
        )
        d_attended = d_windowed.reshape(wins_dev, window, heads_here, head_dim)
        scores_again = (
            jnp.einsum("wqhd,wkhd->whqk", queries, key_rows, preferred_element_type=jnp.float32)
            * score_scale
        )
        probs_again = jnp.exp(jnp.where(allowed, scores_again, MASKED) - log_total)
        d_probs = jnp.einsum(
            "wqhd,wkhd->whqk", d_attended, values, preferred_element_type=jnp.float32
        )
        d_values = jnp.einsum(
            "whqk,wqhd->wkhd",
            probs_again.astype(jnp.bfloat16),
            d_attended,
            preferred_element_type=jnp.float32,
        )
        row_delta = jnp.sum(probs_again * d_probs, axis=-1, keepdims=True)
        d_scores = (probs_again * (d_probs - row_delta)).astype(jnp.bfloat16)
        d_queries = (
            jnp.einsum("whqk,wkhd->wqhd", d_scores, key_rows, preferred_element_type=jnp.float32)
            * score_scale
        )
        d_keys = (
            jnp.einsum("whqk,wqhd->wkhd", d_scores, queries, preferred_element_type=jnp.float32)
            * score_scale
        )
        d_qkv = jnp.concatenate(
            [
                d_queries.astype(jnp.bfloat16).reshape(wins_dev, window, 1, group_width),
                d_keys.astype(jnp.bfloat16).reshape(wins_dev, window, 1, group_width),
                d_values.astype(jnp.bfloat16).reshape(wins_dev, window, 1, group_width),
            ],
            axis=-1,
        )
        d_tokens = lax.all_to_all(d_qkv, "dp", split_axis=1, concat_axis=2, tiled=True).reshape(
            -1, 3 * model_width
        )
        d_start = d_mixed + product_back(d_tokens, w_qkv)
        input_rows.append(d_start.reshape(wins_dev, segment, model_width))
        grad_qkv = grad_qkv + product_outer(start_low, d_tokens)
        grad_out = grad_out + product_outer(returned, d_branch_attn)
        grad_up = grad_up + product_outer(normed_low, d_up_low)
        grad_down = grad_down + product_outer(activated_low, d_branch_ff)
        grad_bias_qkv = grad_bias_qkv + column_sum(d_tokens)
        grad_bias_out = grad_bias_out + column_sum(d_branch_attn)
        grad_bias_up = grad_bias_up + column_sum(d_up_low)
        grad_bias_down = grad_bias_down + column_sum(d_branch_ff)
        norm_grads = [
            norm_grads[0] + d_gain_one,
            norm_grads[1] + d_shift_one,
            norm_grads[2] + d_gain_two,
            norm_grads[3] + d_shift_two,
        ]
        grad_positions = grad_positions + jnp.sum(
            d_start.reshape(wins_dev, segment, model_width), axis=0
        )
    grad_plain = (
        grad_qkv.reshape(model_width, dp_count, 3, group_width)
        .transpose(0, 2, 1, 3)
        .reshape(model_width, 3 * model_width)
    )
    bias_parts = grad_bias_qkv.reshape(dp_count, 3, group_width)
    grad_bias_query = bias_parts[:, 0].reshape(model_width)
    grad_bias_value = bias_parts[:, 2].reshape(model_width)
    grad_stack = jnp.concatenate(
        [
            to_blocks(grad_plain[:, 0:model_width], block_size),
            to_blocks(grad_plain[:, model_width : 2 * model_width], block_size),
            to_blocks(grad_plain[:, 2 * model_width :], block_size),
            to_blocks(grad_out, block_size),
            to_blocks(grad_up, block_size),
            to_blocks(grad_down, block_size),
        ],
        axis=0,
    )
    arranged = grad_stack.reshape(dp_count, owned_blocks, seq_count, row_part, block_size)
    arranged = arranged.transpose(2, 0, 1, 3, 4).reshape(
        seq_count * dp_count * owned_blocks, row_part, block_size
    )
    grad_rows = lax.psum_scatter(arranged, ("seq", "dp"), scatter_dimension=0, tiled=True)
    grad_full, roots_full = (
        lax.all_gather(grad_rows.astype(jnp.bfloat16), "seq", axis=1, tiled=True).astype(
            grad_rows.dtype
        ),
        lax.all_gather(right_roots.astype(jnp.bfloat16), "seq", axis=1, tiled=True).astype(
            right_roots.dtype
        ),
    )
    highest = lax.Precision.HIGHEST
    row_start = seq_index * row_part
    left_new = DECAY * left_stats + (1.0 - DECAY) * jnp.einsum(
        "bij,bkj->bik", grad_rows, grad_full, precision=highest
    )
    column_part = lax.dynamic_slice_in_dim(grad_full, row_start, row_part, 2)
    right_new = DECAY * right_stats + (1.0 - DECAY) * jnp.einsum(
        "bki,bkj->bij", column_part, grad_full, precision=highest
    )
    left_applied = jnp.einsum("bij,bjk->bik", left_roots, grad_full, precision=highest)
    step_rows = jnp.einsum("bij,bjk->bik", left_applied, roots_full, precision=highest)
    weights_new = weights - MATRIX_RATE * step_rows
    vector_terms = jnp.concatenate(
        [
            grad_bias_query,
            grad_bias_value,
            grad_bias_out,
            grad_bias_up,
            grad_bias_down,
            norm_grads[0],
            norm_grads[1],
            norm_grads[2],
            norm_grads[3],
        ]
    )
    vector_grads = lax.psum(vector_terms, ("seq", "dp"))
    position_grads = lax.psum(grad_positions.astype(jnp.bfloat16), "seq").astype(jnp.float32)
    vector_second_new = DECAY * vector_second + (1.0 - DECAY) * vector_grads * vector_grads
    vectors_new = vectors - VECTOR_RATE * vector_grads / (jnp.sqrt(vector_second_new) + ROOT_EPS)
    position_second_new = DECAY * position_second + (1.0 - DECAY) * position_grads * position_grads
    positions_new = positions - VECTOR_RATE * position_grads / (
        jnp.sqrt(position_second_new) + ROOT_EPS
    )
    layer_out = jnp.stack(layer_rows, axis=0)
    input_grad = jnp.stack(input_rows, axis=0)
    return (
        layer_out,
        input_grad,
        grad_rows,
        left_new,
        right_new,
        weights_new,
        vector_grads,
        vector_second_new,
        vectors_new,
        position_grads,
        position_second_new,
        positions_new,
    )


def solution(mesh):
    in_specs = (
        P(None, "seq", "dp", None),
        P(None, "seq", "dp", None),
        P(None, "seq"),
        P("dp", "seq", None),
        P(),
        P("dp", None),
        P("dp", "seq", None),
        P("dp", "seq", None),
        P("dp", "seq", None),
        P("dp", "seq", None),
        P(),
        P("dp", None),
    )
    out_specs = (
        P(None, "seq", "dp", None),
        P(None, "seq", "dp", None),
        P("dp", "seq", None),
        P("dp", "seq", None),
        P("dp", "seq", None),
        P("dp", "seq", None),
        P(),
        P(),
        P(),
        P("dp", None),
        P("dp", None),
        P("dp", None),
    )
    return jax.shard_map(body, mesh=mesh, in_specs=in_specs, out_specs=out_specs, check_vma=False)
```

profile of v0, /device:TPU:0, one launch (start us, length us, event | category | flops | bytes accessed | tf_op | source)
XLA Modules:
  0.0 1010.5 jit_solution(1063434561192250567)
XLA Ops:
  13.6 70.1 %all-gather.9.cloned.1.call-done = bf16[384,32,256]{2,1,0:T(8,128)(2,1)} async-done(((bf16[12,32,256]{2,1,0:T(8,128)(2,1)}), bf16[384,32,256]{2,1,0:T(8,128)(2,1)}) %all-gather.9.cloned.1.call-update) | async-done | bytes 6291472 | tf_op jit(solution)/shard_map/all_gather | solution.py:84
  128.2 52.5 %all-to-all-done = bf16[8,128,4,384]{3,1,0,2:T(8,128)(2,1)S(1)} async-done(((bf16[8,128,4,384]{3,1,0,2:T(8,128)(2,1)}), bf16[8,128,4,384]{3,1,0,2:T(8,128)(2,1)S(1)}, u32[]{:S(2)}, u32[]{:S(2)}) %all-to-all-start) | async-done | bytes 3145760 | tf_op jit(solution)/shard_map/all_to_all | solution.py:148
  195.5 9.1 fusion.99
  204.7 8.3 fusion
  222.0 34.1 %all-to-all-done.2 = bf16[8,128,4,384]{3,1,0,2:T(8,128)(2,1)} async-done(((bf16[8,128,4,384]{3,1,0,2:T(8,128)(2,1)}), bf16[8,128,4,384]{3,1,0,2:T(8,128)(2,1)}, u32[]{:S(2)}, u32[]{:S(2)}) %all-to-all-start.2) | async-done | bytes 3145760 | tf_op jit(solution)/shard_map/all_to_all | solution.py:148
  267.8 9.1 fusion.101
  285.3 8.5 fusion.49
  337.6 40.8 %multiply_convert_fusion.3 = (bf16[1024,2048]{1,0:T(8,128)(2,1)S(1)}, f32[1024,2048]{1,0:T(8,128)}, bf16[1024,2048]{1,0:T(8,128)(2,1)S(1)}, f32[1024,2048]{1,0:T(8,128)}, f32[1024,2048]{1,0:T(8,128)}) fusion(f32[2048]{0:T(1024)S(1)} %copy-done.93, f32[1024,2048]{1,0:T(8,128)S(1)} %fusion.80, bf16[512,2048]{1,0:T(8,128)(2,1)S(1)} %bitcast.395, ...), kind=kOutput, calls=%fused_computation.41 | convolution fusion | flops 2426929152 | bytes 46157824 | tf_op jit(solution)/shard_map/dot_general | solution.py:41
  393.0 9.5 convert_reduce_fusion
  405.7 9.5 convert_reduce_fusion.1
  439.5 20.5 %all-to-all-done.4 = bf16[8,128,4,128]{3,1,0,2:T(8,128)(2,1)} async-done(((bf16[8,128,4,128]{3,1,0,2:T(8,128)(2,1)}), bf16[8,128,4,128]{3,1,0,2:T(8,128)(2,1)}, u32[]{:S(2)}, u32[]{:S(2)}) %all-to-all-start.4) | async-done | bytes 1048608 | tf_op jit(solution)/shard_map/all_to_all | solution.py:202
  467.2 13.9 %multiply_reduce_fusion.1 = (f32[8,2,512]{2,1,0:T(2,128)S(1)}, f32[8,2,512,512]{2,3,1,0:T(8,128)}) fusion(f32[8,2,512,512]{2,3,1,0:T(8,128)} %get-tuple-element.100, f32[8,2,512]{2,1,0:T(2,128)S(1)} %bitcast.423, bf16[8,512,2,64]{1,3,2,0:T(8,128)(2,1)} %reshape.646, bf16[8,512,2,64]{1,3,2,0:T(8,128)(2,1)} %bitcast.375), kind=kOutput, calls=%fused_computation.4 | convolution fusion | flops 549445632 | bytes 35717120 | tf_op jit(solution)/shard_map/wqhd,wkhd->whqk/dot_general | solution.py:215
  484.2 8.4 multiply_convert_fusion.1
  504.9 8.5 fusion.51
  525.7 13.9 %multiply_reduce_fusion = (f32[8,2,512]{2,1,0:T(2,128)S(1)}, f32[8,2,512,512]{2,3,1,0:T(8,128)}) fusion(f32[8,2,512,512]{2,3,1,0:T(8,128)} %get-tuple-element.104, f32[8,2,512]{2,1,0:T(2,128)S(1)} %bitcast.421, bf16[8,512,2,64]{1,3,2,0:T(8,128)(2,1)} %reshape.652, bf16[8,512,2,64]{1,3,2,0:T(8,128)(2,1)} %bitcast.373), kind=kOutput, calls=%fused_computation.1 | convolution fusion | flops 549445632 | bytes 35717120 | tf_op jit(solution)/shard_map/wqhd,wkhd->whqk/dot_general | solution.py:215
  542.8 8.4 multiply_convert_fusion
  563.5 8.5 fusion.54
  576.1 16.5 %all-to-all-done.5 = bf16[8,512,1,384]{3,0,2,1:T(8,128)(2,1)} async-done(((bf16[8,512,1,384]{3,0,2,1:T(8,128)(2,1)}), bf16[8,512,1,384]{3,0,2,1:T(8,128)(2,1)}, u32[]{:S(2)}, u32[]{:S(2)}) %all-to-all-start.5) | async-done | bytes 3145760 | tf_op jit(solution)/shard_map/all_to_all | solution.py:242
  638.4 29.1 %all-to-all-done.7 = bf16[8,512,1,384]{3,0,2,1:T(8,128)(2,1)} async-done(((bf16[8,512,1,384]{3,0,2,1:T(8,128)(2,1)}), bf16[8,512,1,384]{3,0,2,1:T(8,128)(2,1)}, u32[]{:S(2)}, u32[]{:S(2)}) %all-to-all-start.7) | async-done | bytes 3145760 | tf_op jit(solution)/shard_map/all_to_all | solution.py:242
  721.7 11.9 %copy.172 = f32[8,4,12,32,256]{4,3,2,1,0:T(8,128)} copy(f32[8,4,12,32,256]{4,3,0,2,1:T(8,128)} %bitcast.342) | data formatting | bytes 25165824 | tf_op jit(solution)/shard_map/transpose | solution.py:284
  754.2 133.6 %reduce-scatter.2.cloned.1.call-done = f32[12,32,256]{2,1,0:T(8,128)} async-done(((f32[384,32,256]{2,1,0:T(8,128)}), f32[12,32,256]{2,1,0:T(8,128)}) %reduce-scatter.2.cloned.1.call-update) | async-done | bytes 393232 | tf_op jit(solution)/shard_map/reduce_scatter | solution.py:287
  910.2 40.1 %psum.14 = f32[6144]{0:T(1024)S(1)} all-reduce(f32[6144]{0:T(1024)} %constant_dynamic-update-slice_fusion.7), channel_id=1, replica_groups=mesh['seq'=8,'dp'=4] {'seq','dp'}, use_global_device_ids=true, to_apply=%region_39.40 | all-reduce | flops 6144 | bytes 49152 | tf_op jit(solution)/shard_map/psum | solution.py:321
  957.3 13.8 %all-gather.5.cloned.1.call-done = bf16[12,256,256]{2,1,0:T(8,128)(2,1)} async-done(((bf16[12,32,256]{2,1,0:T(8,128)(2,1)}), bf16[12,256,256]{2,1,0:T(8,128)(2,1)}) %all-gather.5.cloned.1.call-update) | async-done | bytes 1572880 | tf_op jit(solution)/shard_map/all_gather | solution.py:289
  976.8 22.4 %all-gather.7.cloned.1.call-done = bf16[12,256,256]{2,1,0:T(8,128)(2,1)} async-done(((bf16[12,32,256]{2,1,0:T(8,128)(2,1)}), bf16[12,256,256]{2,1,0:T(8,128)(2,1)}) %all-gather.7.cloned.1.call-update) | async-done | bytes 1572880 | tf_op jit(solution)/shard_map/all_gather | solution.py:292
  (451 shorter events, 393.9 us)
Async XLA Ops:
  7.2 964.0 %copy-start = (f32[12,32,256]{2,1,0:T(8,128)S(1)}, f32[12,32,256]{2,1,0:T(8,128)}, u32[]{:S(2)}) copy-start(f32[12,32,256]{2,1,0:T(8,128)} %param.20) | copy-start | bytes 1179652
  7.2 76.6 %all-gather.9.cloned.1.call-start = ((), (), s32[]{:S(2)}) async-start(), calls=%async_computation.13 | async-start | bytes 6488064 | tf_op jit(solution)/shard_map/all_gather | solution.py:84
  10.6 83.0 %copy-start.94 = (f32[1536]{0:T(1024)}, f32[1536]{0:T(1024)S(1)}, u32[]{:S(2)}) copy-start(f32[1536]{0:T(1024)S(1)} %add.302) | copy-start | bytes 18436
  13.6 80.0 %copy-start.53 = (bf16[8,128,512]{2,1,0:T(8,128)(2,1)}, bf16[8,128,512]{2,1,0:T(8,128)(2,1)S(1)}, u32[]{:S(2)}) copy-start(bf16[8,128,512]{2,1,0:T(8,128)(2,1)S(1)} %get-tuple-element.66) | copy-start | bytes 3145732
  105.5 75.2 %all-to-all-start = ((bf16[8,128,4,384]{3,1,0,2:T(8,128)(2,1)}), bf16[8,128,4,384]{3,1,0,2:T(8,128)(2,1)S(1)}, u32[]{:S(2)}, u32[]{:S(2)}) async-start(bf16[8,128,4,384]{3,1,0,2:T(8,128)(2,1)} %copy.123), calls=%async_computation | async-start | bytes 6291456 | tf_op jit(solution)/shard_map/all_to_all | solution.py:148
  112.0 189.9 %copy-start.95 = (s32[8]{0:T(128)}, s32[8]{0:T(128)S(1)}, u32[]{:S(2)}) copy-start(s32[8]{0:T(128)S(1)} %get-tuple-element.95) | copy-start | bytes 100
  180.7 75.5 %all-to-all-start.2 = ((bf16[8,128,4,384]{3,1,0,2:T(8,128)(2,1)}), bf16[8,128,4,384]{3,1,0,2:T(8,128)(2,1)}, u32[]{:S(2)}, u32[]{:S(2)}) async-start(bf16[8,128,4,384]{3,1,0,2:T(8,128)(2,1)} %copy.135), calls=%async_computation.2 | async-start | bytes 6291456 | tf_op jit(solution)/shard_map/all_to_all | solution.py:148
  256.1 40.2 %all-to-all-start.1 = ((bf16[8,512,1,128]{3,0,2,1:T(8,128)(2,1)}), bf16[8,512,1,128]{3,0,2,1:T(8,128)(2,1)}, u32[]{:S(2)}, u32[]{:S(2)}) async-start(bf16[8,512,1,128]{3,0,2,1:T(8,128)(2,1)} %copy.129), calls=%async_computation.1 | async-start | bytes 2097152 | tf_op jit(solution)/shard_map/all_to_all | solution.py:178
  296.4 30.2 %all-to-all-start.3 = ((bf16[8,512,1,128]{3,0,2,1:T(8,128)(2,1)}), bf16[8,512,1,128]{3,0,2,1:T(8,128)(2,1)}, u32[]{:S(2)}, u32[]{:S(2)}) async-start(bf16[8,512,1,128]{3,0,2,1:T(8,128)(2,1)} %copy.141), calls=%async_computation.3 | async-start | bytes 2097152 | tf_op jit(solution)/shard_map/all_to_all | solution.py:178
  324.1 94.8 %copy-start.3 = (f32[1024,512]{1,0:T(8,128)}, f32[1024,512]{1,0:T(8,128)S(1)}, u32[]{:S(2)}) copy-start(f32[1024,512]{1,0:T(8,128)S(1)} %get-tuple-element.102) | copy-start | bytes 6291460
  333.8 85.1 %copy-start.5 = (f32[1024,512]{1,0:T(8,128)}, f32[1024,512]{1,0:T(8,128)S(1)}, u32[]{:S(2)}) copy-start(f32[1024,512]{1,0:T(8,128)S(1)} %get-tuple-element.106) | copy-start | bytes 6291460
  430.5 29.5 %all-to-all-start.4 = ((bf16[8,128,4,128]{3,1,0,2:T(8,128)(2,1)}), bf16[8,128,4,128]{3,1,0,2:T(8,128)(2,1)}, u32[]{:S(2)}, u32[]{:S(2)}) async-start(bf16[8,128,4,128]{3,1,0,2:T(8,128)(2,1)} %copy.144), calls=%async_computation.4 | async-start | bytes 2097152 | tf_op jit(solution)/shard_map/all_to_all | solution.py:202
  434.8 46.4 %copy-start.61 = (f32[2,8,512]{2,1,0:T(8,128)}, f32[2,8,512]{2,1,0:T(8,128)S(1)}, u32[]{:S(2)}) copy-start(f32[2,8,512]{2,1,0:T(8,128)S(1)} %log_add_fusion.1) | copy-start | bytes 98308
  460.0 57.5 %all-to-all-start.6 = ((bf16[8,128,4,128]{3,1,0,2:T(8,128)(2,1)}), bf16[8,128,4,128]{3,1,0,2:T(8,128)(2,1)}, u32[]{:S(2)}, u32[]{:S(2)}) async-start(bf16[8,128,4,128]{3,1,0,2:T(8,128)(2,1)} %copy.154), calls=%async_computation.6 | async-start | bytes 2097152 | tf_op jit(solution)/shard_map/all_to_all | solution.py:202
  517.5 75.0 %all-to-all-start.5 = ((bf16[8,512,1,384]{3,0,2,1:T(8,128)(2,1)}), bf16[8,512,1,384]{3,0,2,1:T(8,128)(2,1)}, u32[]{:S(2)}, u32[]{:S(2)}) async-start(bf16[8,512,1,384]{3,0,2,1:T(8,128)(2,1)} %pad_maximum_fusion.1), calls=%async_computation.5 | async-start | bytes 6291456 | tf_op jit(solution)/shard_map/all_to_all | solution.py:242
  592.6 74.9 %all-to-all-start.7 = ((bf16[8,512,1,384]{3,0,2,1:T(8,128)(2,1)}), bf16[8,512,1,384]{3,0,2,1:T(8,128)(2,1)}, u32[]{:S(2)}, u32[]{:S(2)}) async-start(bf16[8,512,1,384]{3,0,2,1:T(8,128)(2,1)} %pad_maximum_fusion.2), calls=%async_computation.7 | async-start | bytes 6291456 | tf_op jit(solution)/shard_map/all_to_all | solution.py:242
  597.3 290.5 %reduce-scatter.2.cloned.1.call-start = ((), (), s32[]{:S(2)}) async-start(), calls=%async_computation.9 | async-start | bytes 12976128 | tf_op jit(solution)/shard_map/reduce_scatter | solution.py:287
  733.7 221.6 %all-reduce.2.cloned.1.call-start = ((), (), s32[]{:S(2)}) async-start(), calls=%async_computation.12 | async-start | bytes 262144 | tf_op jit(solution)/shard_map/psum | solution.py:322
  749.7 141.6 %copy-start.96 = (s32[8]{0:T(128)S(1)}, s32[8]{0:T(128)}, u32[]{:S(2)}) copy-start(s32[8]{0:T(128)} %copy-done.95) | copy-start | bytes 100
  749.7 141.6 %copy-start.99 = (s32[8]{0:T(128)S(1)}, s32[8]{0:T(128)}, u32[]{:S(2)}) copy-start(s32[8]{0:T(128)} %copy-done.97) | copy-start | bytes 100
  754.1 217.0 %all-gather.5.cloned.1.call-start = ((), (), s32[]{:S(2)}) async-start(), calls=%async_computation.10 | async-start | bytes 1769472 | tf_op jit(solution)/shard_map/all_gather | solution.py:289
  889.5 109.7 %all-gather.7.cloned.1.call-start = ((), (), s32[]{:S(2)}) async-start(), calls=%async_computation.11 | async-start | bytes 1769472 | tf_op jit(solution)/shard_map/all_gather | solution.py:292
  897.9 52.4 %copy-start.20 = (f32[1024,512]{1,0:T(8,128)S(1)}, f32[1024,512]{1,0:T(8,128)}, u32[]{:S(2)}) copy-start(f32[1024,512]{1,0:T(8,128)} %add_add_fusion.8) | copy-start | bytes 6291460
  955.3 43.9 %copy-start.50 = (f32[12,32,256]{2,1,0:T(8,128)S(1)}, f32[12,32,256]{2,1,0:T(8,128)}, u32[]{:S(2)}) copy-start(f32[12,32,256]{2,1,0:T(8,128)} %param.15) | copy-start | bytes 1179652
  (114 other events, 881.0 us)
Sparse Core Ops, SparseCore 0:
  11.5 72.2 all-gather.8
  733.8 153.9 reduce-scatter.1
  891.6 51.9 all-reduce.1
  946.0 25.0 all-gather.4
  973.5 25.6 all-gather.6
where the time goes:
time: 1020 us; the launch traced here: 1010 us
  waiting for transfers between devices  395 us (39%)
  matrix products  231 us (23%)
  local copies, waits for them, and re-layouts  187 us (18%)
  other arithmetic  104 us (10%)
  blocking collectives  40.1 us (4%)
  starting transfers between devices  37.5 us (4%)
  between operations  15.6 us (2%)
    reduce_scatter x1, waiting for transfers between devices, body(): lax.psum_scatter(arranged, ('seq', 'dp'), scatter_dimension=0, tiled=True)  134 us
    all_to_all x2, waiting for transfers between devices, body(): lax.all_to_all(qkv_rows.reshape(wins_dev, segment, dp_count, 3 * group_wi...  86.6 us
    all_gather x1, waiting for transfers between devices, body(): lax.all_gather(weights[None].astype(jnp.bfloat16), ('seq', 'dp'), axis=0,...  70.1 us
    dot_general x8, matrix products, product_low(): return jnp.dot(left_rows, right_matrix, preferred_element_type=jnp.float32)  63.2 us
    all_to_all x2, waiting for transfers between devices, body(): lax.all_to_all(d_qkv, 'dp', split_axis=1, concat_axis=2, tiled=True)  45.6 us
    unnamed x261, local copies, waits for them, and re-layouts  40.7 us
    dot_general x8, matrix products, product_back(): jnp.einsum('re,de->rd', left_rows, right_matrix, preferred_element_type=j...  40.2 us
    psum x1, blocking collectives, body(): vector_grads = lax.psum(vector_terms, ('seq', 'dp'))  40.1 us
  transfers between devices with their start and end apart: 13, of which 10 were waited for; matrix products, arithmetic and copies ran while one was open for 31% of the time, Pallas kernels for 0%

commit v1 on v0

v1 whole, which is shorter than its diff:
```python
import functools

import jax
import jax.numpy as jnp
from jax import lax
from jax.experimental import pallas as pl
from jax.experimental.pallas import tpu as pltpu
from jax.sharding import PartitionSpec as P

HEADS = 8
FF = 2048
WIN = 512
D = 512
BLK = 256
QKV_BLOCKS = 12
REST_BLOCKS = 36
HEAD_DIM = D // HEADS
PAIR = 2 * HEAD_DIM
PAIRS = HEADS // 2
FF_CHUNKS = FF // BLK
ROWS_VEC = 16

NORM_EPS = 1e-05
ROOT_EPS = 1e-08
DECAY = 0.5
MATRIX_RATE = 0.5
VECTOR_RATE = 0.2
MASKED = -1e30
SCALE = HEAD_DIM ** (-0.5)
ROOT_HALF = 0.7071067811865476
DENSITY = 0.3989422804014327

F32 = jnp.float32
BF16 = jnp.bfloat16


def dot_nn(left, right):
    return lax.dot_general(left, right, (((1,), (0,)), ((), ())), preferred_element_type=F32)


def dot_nt(left, right):
    return lax.dot_general(left, right, (((1,), (1,)), ((), ())), preferred_element_type=F32)


def load_segments(dst, lead, parts, me, seg):
    for s, part in enumerate(parts):
        rows = pl.ds(pl.multiple_of((me ^ s) * seg, seg), seg)
        if lead:
            dst[0, rows, :] = part[0]
        else:
            dst[rows, :] = part[0]


def fill_qkv_matrix(full, stack):
    side = D // BLK
    for b in range(QKV_BLOCKS):
        m, i, j = b // (side * side), (b // side) % side, b % side
        full[BLK * i : BLK * (i + 1), D * m + BLK * j : D * m + BLK * (j + 1)] = stack[b]


def fill_mask(mask, length):
    for i in range(WIN // BLK):
        keys = lax.broadcasted_iota(jnp.int32, (BLK, WIN), 0) + BLK * i
        queries = lax.broadcasted_iota(jnp.int32, (BLK, WIN), 1)
        keep = (keys <= queries) & (keys < length)
        mask[BLK * i : BLK * (i + 1), :] = jnp.where(keep, 0.0, MASKED).astype(F32)


def half_marks():
    lane = lax.broadcasted_iota(jnp.int32, (1, PAIR), 1)
    low = jnp.where(lane < HEAD_DIM, 1.0, 0.0)
    return (low.astype(BF16), (1.0 - low).astype(BF16))


def attention_kernel(dp, seg, meta, *refs):
    parts = refs[:dp]
    stack, bias, h_ref, qkv_ref, o_ref, lse_ref, full, mask = refs[dp:]
    step = pl.program_id(0)
    me = meta[0]

    @pl.when(step == 0)
    def _():
        fill_qkv_matrix(full, stack)

    load_segments(h_ref, True, parts, me, seg)
    hidden = h_ref[0]
    for m in range(3):
        cols = slice(D * m, D * (m + 1))
        rows = dot_nn(hidden, full[:, cols])
        if m != 1:
            rows = rows + bias[(m // 2) : (m // 2) + 1, :]
        qkv_ref[0, :, cols] = rows.astype(BF16)
    fill_mask(mask, meta[1 + step])
    marks = half_marks()
    for p in range(PAIRS):
        at = PAIR * p
        q8 = qkv_ref[0, :, at : at + PAIR] * jnp.asarray(SCALE, BF16)
        key = qkv_ref[0, :, D + at : D + at + PAIR]
        val_t = jnp.transpose(qkv_ref[0, :, 2 * D + at : 2 * D + at + PAIR])
        pieces = []
        for h in range(2):
            key_h = key * marks[h]
            row = 2 * p + h
            blocks = []
            for qb in range(WIN // BLK):
                cols = slice(BLK * qb, BLK * (qb + 1))
                span = BLK * (qb + 1)
                s_t = dot_nt(key_h[:span], q8[cols]) + mask[:span, cols]
                top = jnp.max(s_t, axis=0, keepdims=True)
                expo = jnp.exp(s_t - top)
                total = jnp.sum(expo, axis=0, keepdims=True)
                probs = (expo * (1.0 / total)).astype(BF16)
                lse_ref[0, row : row + 1, cols] = top + jnp.log(total)
                blocks.append(dot_nn(val_t[HEAD_DIM * h : HEAD_DIM * (h + 1), :span], probs))
            pieces.append(jnp.concatenate(blocks, axis=1))
        o_t = jnp.concatenate(pieces, axis=0)
        o_ref[0, :, at : at + PAIR] = jnp.transpose(o_t).astype(BF16)


def attention_back_kernel(dp, seg, first, meta, *refs):
    stack, h_ref, qkv_ref, do_ref, lse_ref, da_ref = refs[:6]
    refs = refs[6:]
    if not first:
        prev, refs = refs[0], refs[1:]
    dx_refs, refs = refs[:dp], refs[dp:]
    dw_ref, db_ref, full, mask, dqkv, acc, dx = refs
    step = pl.program_id(0)
    me = meta[0]
    side = D // BLK

    @pl.when(step == 0)
    def _():
        fill_qkv_matrix(full, stack)
        if first:
            acc[...] = jnp.zeros_like(acc)
        else:
            for b in range(QKV_BLOCKS):
                m, i, j = b // (side * side), (b // side) % side, b % side
                acc[BLK * i : BLK * (i + 1), D * m + BLK * j : D * m + BLK * (j + 1)] = prev[
                    b
                ].astype(F32)
        db_ref[...] = jnp.zeros_like(db_ref)

    fill_mask(mask, meta[1 + step])
    marks = half_marks()
    for p in range(PAIRS):
        at = PAIR * p
        q8 = qkv_ref[0, :, at : at + PAIR] * jnp.asarray(SCALE, BF16)
        key = qkv_ref[0, :, D + at : D + at + PAIR]
        val = qkv_ref[0, :, 2 * D + at : 2 * D + at + PAIR]
        d_o = do_ref[0, :, at : at + PAIR]
        key_t = jnp.transpose(key)
        dq_pieces, dk_pieces, dv_pieces = [], [], []
        for h in range(2):
            key_h = key * marks[h]
            val_h = val * marks[h]
            row = 2 * p + h
            dq_blocks = []
            dk_sum, dv_sum = None, None
            for qb in reversed(range(WIN // BLK)):
                cols = slice(BLK * qb, BLK * (qb + 1))
                span = BLK * (qb + 1)
                s_t = dot_nt(key_h[:span], q8[cols]) + mask[:span, cols]
                probs = jnp.exp(s_t - lse_ref[0, row : row + 1, cols])
                d_probs = dot_nt(val_h[:span], d_o[cols])
                delta = jnp.sum(probs * d_probs, axis=0, keepdims=True)
                d_s = (probs * (d_probs - delta)).astype(BF16)
                dv_part = dot_nn(probs.astype(BF16), d_o[cols])
                dk_part = dot_nn(d_s, q8[cols])
                dq_blocks.append(dot_nn(key_t[HEAD_DIM * h : HEAD_DIM * (h + 1), :span], d_s))
                if dv_sum is None:
                    dv_sum, dk_sum = dv_part, dk_part
                else:
                    dv_sum = jnp.concatenate([dv_sum[:span] + dv_part, dv_sum[span:]], axis=0)
                    dk_sum = jnp.concatenate([dk_sum[:span] + dk_part, dk_sum[span:]], axis=0)
            dq_pieces.append(jnp.concatenate(dq_blocks[::-1], axis=1))
            dk_pieces.append(dk_sum)
            dv_pieces.append(dv_sum)
        lane = lax.broadcasted_iota(jnp.int32, (WIN, PAIR), 1) < HEAD_DIM
        dq = jnp.transpose(jnp.concatenate(dq_pieces, axis=0)) * SCALE
        dk = jnp.where(lane, dk_pieces[0], dk_pieces[1])
        dv = jnp.where(lane, dv_pieces[0], dv_pieces[1])
        dqkv[:, at : at + PAIR] = dq.astype(BF16)
        dqkv[:, D + at : D + at + PAIR] = dk.astype(BF16)
        dqkv[:, 2 * D + at : 2 * D + at + PAIR] = dv.astype(BF16)
    h_t = jnp.transpose(h_ref[0])
    for m in range(3):
        cols = slice(D * m, D * (m + 1))
        rows = dqkv[:, cols]
        acc[:, cols] += dot_nn(h_t, rows)
        if m != 1:
            db_ref[(m // 2) : (m // 2) + 1, :] += jnp.sum(
                rows.astype(F32), axis=0, keepdims=True
            )
    total = da_ref[0]
    for m in range(3):
        cols = slice(D * m, D * (m + 1))
        total = total + dot_nt(dqkv[:, cols], full[:, cols])
    dx[...] = total.astype(BF16)
    for s in range(dp):
        dx_refs[s][0] = dx[pl.ds(pl.multiple_of((me ^ s) * seg, seg), seg), :]

    @pl.when(step == pl.num_programs(0) - 1)
    def _():
        for b in range(QKV_BLOCKS):
            m, i, j = b // (side * side), (b // side) % side, b % side
            dw_ref[b] = acc[
                BLK * i : BLK * (i + 1), D * m + BLK * j : D * m + BLK * (j + 1)
            ].astype(BF16)


def normal_parts(u):
    size = jnp.abs(u)
    t = 1.0 / (1.0 + (0.3275911 * ROOT_HALF) * size)
    expo = jnp.exp(-0.5 * (u * u))
    poly = t * (
        0.5 * 0.254829592
        + t
        * (
            -0.5 * 0.284496736
            + t * (0.5 * 1.421413741 + t * (-0.5 * 1.453152027 + t * (0.5 * 1.061405429)))
        )
    )
    tail = poly * expo
    return jnp.where(u >= 0.0, 1.0 - tail, tail), expo


def norm_stats(rows):
    mean = jnp.mean(rows, axis=1, keepdims=True)
    centered = rows - mean
    spread = jnp.mean(centered * centered, axis=1, keepdims=True)
    inverse = lax.rsqrt(spread + NORM_EPS)
    return centered * inverse, inverse


def norm_back(d_rows, normal, inverse):
    mean_d = jnp.mean(d_rows, axis=1, keepdims=True)
    mean_dn = jnp.mean(d_rows * normal, axis=1, keepdims=True)
    return inverse * (d_rows - mean_d - normal * mean_dn)


def ffn_kernel(dp, seg, tokens, first, meta, *refs):
    cots, refs = refs[:dp], refs[dp:]
    h_ref, o_ref, stack, vec = refs[:4]
    refs = refs[4:]
    if not first:
        prev, refs = refs[0], refs[1:]
    out_refs, refs = refs[:dp], refs[dp:]
    da_ref, do_ref, dw_ref, vg_ref, acc, z_ref, gp_ref, buf, w_out = refs
    step = pl.program_id(0)
    me = meta[0]
    length = meta[1 + step]
    side = D // BLK
    up_at = side * side
    down_at = up_at + side * FF_CHUNKS

    @pl.when(step == 0)
    def _():
        for b in range(side * side):
            i, j = b // side, b % side
            w_out[BLK * i : BLK * (i + 1), BLK * j : BLK * (j + 1)] = stack[b]
        for b in range(REST_BLOCKS):
            if first:
                acc[b] = jnp.zeros((BLK, BLK), F32)
            elif b >= down_at:
                acc[b] = jnp.transpose(prev[b].astype(F32))
            else:
                acc[b] = prev[b].astype(F32)
        vg_ref[...] = jnp.zeros_like(vg_ref)

    def add_row(row, values, at=0):
        vg_ref[row : row + 1, at : at + values.shape[1]] += jnp.sum(
            values.astype(F32), axis=0, keepdims=True
        )

    bias_out, bias_down = vec[2:3, :], vec[7:8, :]
    gain_one, shift_one = vec[8:9, :], vec[9:10, :]
    gain_two, shift_two = vec[10:11, :], vec[11:12, :]
    attended = o_ref[0]
    mixed = h_ref[0].astype(F32) + (dot_nn(attended, w_out[...]) + bias_out)
    n_one, inv_one = norm_stats(mixed)
    normed = n_one * gain_one + shift_one
    normed_low = normed.astype(BF16)
    summed = normed + bias_down
    left, right = normed_low[:, :BLK], normed_low[:, BLK:]
    f_parts = [summed[:, :BLK], summed[:, BLK:]]
    for c in range(FF_CHUNKS):
        cols = slice(BLK * c, BLK * (c + 1))
        bias_up = vec[3 + c // 2 : 4 + c // 2, BLK * (c % 2) : BLK * (c % 2) + BLK]
        u = dot_nn(left, stack[up_at + c]) + dot_nn(right, stack[up_at + FF_CHUNKS + c]) + bias_up
        phi, expo = normal_parts(u)
        z = (u * phi).astype(BF16)
        z_ref[:, cols] = z
        gp_ref[:, cols] = phi + (u * expo) * DENSITY
        for j in range(side):
            f_parts[j] = f_parts[j] + dot_nn(z, stack[down_at + side * c + j])
    n_two, inv_two = norm_stats(jnp.concatenate(f_parts, axis=1))
    buf[...] = (n_two * gain_two + shift_two).astype(BF16)
    for s in range(dp):
        out_refs[s][0] = buf[pl.ds(pl.multiple_of((me ^ s) * seg, seg), seg), :]

    load_segments(buf, False, cots, me, seg)
    places = lax.broadcasted_iota(jnp.int32, (WIN, 1), 0)
    valid = jnp.where(places < length, 1.0 / tokens, 0.0).astype(F32)
    seed = buf[...].astype(F32) * valid
    add_row(10, seed * n_two)
    add_row(11, seed)
    d_summed = norm_back(seed * gain_two, n_two, inv_two)
    d_ff = d_summed.astype(BF16)
    add_row(7, d_ff)
    d_ff_t = jnp.transpose(d_ff)
    normed_t = jnp.transpose(normed_low)
    d_left, d_right = d_ff[:, :BLK], d_ff[:, BLK:]
    d_normed = [d_summed[:, :BLK], d_summed[:, BLK:]]
    for c in range(FF_CHUNKS):
        cols = slice(BLK * c, BLK * (c + 1))
        d_z = dot_nt(d_left, stack[down_at + side * c]) + dot_nt(
            d_right, stack[down_at + side * c + 1]
        )
        d_u = (d_z * gp_ref[:, cols]).astype(BF16)
        add_row(3 + c // 2, d_u, BLK * (c % 2))
        z = z_ref[:, cols]
        for j in range(side):
            rows = slice(BLK * j, BLK * (j + 1))
            acc[down_at + side * c + j] += dot_nn(d_ff_t[rows], z)
            acc[up_at + FF_CHUNKS * j + c] += dot_nn(normed_t[rows], d_u)
            d_normed[j] = d_normed[j] + dot_nt(d_u, stack[up_at + FF_CHUNKS * j + c])
    d_norm_rows = jnp.concatenate(d_normed, axis=1)
    add_row(8, d_norm_rows * n_one)
    add_row(9, d_norm_rows)
    d_mixed = norm_back(d_norm_rows * gain_one, n_one, inv_one)
    da_ref[0] = d_mixed
    d_branch = d_mixed.astype(BF16)
    add_row(2, d_branch)
    o_t = jnp.transpose(attended)
    for i in range(side):
        for j in range(side):
            acc[side * i + j] += dot_nn(
                o_t[BLK * i : BLK * (i + 1)], d_branch[:, BLK * j : BLK * (j + 1)]
            )
    do_ref[0] = dot_nt(d_branch, w_out[...]).astype(BF16)

    @pl.when(step == pl.num_programs(0) - 1)
    def _():
        for b in range(REST_BLOCKS):
            block = acc[b]
            if b >= down_at:
                block = jnp.transpose(block)
            dw_ref[b] = block.astype(BF16)


def whole_spec(shape, single=True):
    zeros = (0,) * len(shape)
    if single:
        return pl.BlockSpec(shape, lambda w, m: zeros, pipeline_mode=pl.Buffered(1))
    return pl.BlockSpec(shape, lambda w, m: zeros)


def window_spec(*shape):
    zeros = (0,) * len(shape)
    return pl.BlockSpec((1,) + shape, lambda w, m: (w,) + zeros)


def run_kernel(kernel, wins, meta, ins, in_specs, out_shape, out_specs, scratch, flops, moved):
    return pl.pallas_call(
        kernel,
        grid_spec=pltpu.PrefetchScalarGridSpec(
            num_scalar_prefetch=1,
            grid=(wins,),
            in_specs=in_specs,
            out_specs=out_specs,
            scratch_shapes=scratch,
        ),
        out_shape=out_shape,
        compiler_params=pltpu.CompilerParams(
            dimension_semantics=("arbitrary",), vmem_limit_bytes=56 * 1024 * 1024
        ),
        cost_estimate=pl.CostEstimate(
            flops=flops, bytes_accessed=moved, transcendentals=wins * WIN * FF
        ),
    )(meta, *ins)


def call_attention(dp, seg, meta, parts, stack, bias):
    wins = parts[0].shape[0]
    shape = jax.ShapeDtypeStruct
    return run_kernel(
        functools.partial(attention_kernel, dp, seg),
        wins,
        meta,
        [*parts, stack, bias],
        [window_spec(seg, D)] * dp + [whole_spec(stack.shape), whole_spec(bias.shape)],
        [
            shape((wins, WIN, D), BF16),
            shape((wins, WIN, 3 * D), BF16),
            shape((wins, WIN, D), BF16),
            shape((wins, HEADS, WIN), F32),
        ],
        [
            window_spec(WIN, D),
            window_spec(WIN, 3 * D),
            window_spec(WIN, D),
            window_spec(HEADS, WIN),
        ],
        [pltpu.VMEM((D, 3 * D), BF16), pltpu.VMEM((WIN, WIN), F32)],
        wins * 4_000_000_000,
        wins * 4_000_000,
    )


def call_ffn(dp, seg, tokens, meta, cots, hidden, attended, stack, vec, prev):
    wins = hidden.shape[0]
    shape = jax.ShapeDtypeStruct
    first = prev is None
    ins = [*cots, hidden, attended, stack, vec]
    specs = [window_spec(seg, D)] * dp + [
        window_spec(WIN, D),
        window_spec(WIN, D),
        whole_spec(stack.shape),
        whole_spec(vec.shape),
    ]
    if not first:
        ins.append(prev)
        specs.append(whole_spec(prev.shape))
    return run_kernel(
        functools.partial(ffn_kernel, dp, seg, tokens, first),
        wins,
        meta,
        ins,
        specs,
        [shape((wins, seg, D), BF16)] * dp
        + [
            shape((wins, WIN, D), F32),
            shape((wins, WIN, D), BF16),
            shape((REST_BLOCKS, BLK, BLK), BF16),
            shape((ROWS_VEC, D), F32),
        ],
        [window_spec(seg, D)] * dp
        + [
            window_spec(WIN, D),
            window_spec(WIN, D),
            whole_spec((REST_BLOCKS, BLK, BLK), False),
            whole_spec((ROWS_VEC, D), False),
        ],
        [
            pltpu.VMEM((REST_BLOCKS, BLK, BLK), F32),
            pltpu.VMEM((WIN, FF), BF16),
            pltpu.VMEM((WIN, FF), F32),
            pltpu.VMEM((WIN, D), BF16),
            pltpu.VMEM((D, D), BF16),
        ],
        wins * 8_000_000_000,
        wins * 12_000_000,
    )


def call_attention_back(dp, seg, meta, stack, hidden, qkv, d_o, lse, d_mixed, prev):
    wins = hidden.shape[0]
    shape = jax.ShapeDtypeStruct
    first = prev is None
    ins = [stack, hidden, qkv, d_o, lse, d_mixed]
    specs = [
        whole_spec(stack.shape),
        window_spec(WIN, D),
        window_spec(WIN, 3 * D),
        window_spec(WIN, D),
        window_spec(HEADS, WIN),
        window_spec(WIN, D),
    ]
    if not first:
        ins.append(prev)
        specs.append(whole_spec(prev.shape))
    return run_kernel(
        functools.partial(attention_back_kernel, dp, seg, first),
        wins,
        meta,
        ins,
        specs,
        [shape((wins, seg, D), BF16)] * dp
        + [shape((QKV_BLOCKS, BLK, BLK), BF16), shape((8, D), F32)],
        [window_spec(seg, D)] * dp
        + [whole_spec((QKV_BLOCKS, BLK, BLK), False), whole_spec((8, D), False)],
        [
            pltpu.VMEM((D, 3 * D), BF16),
            pltpu.VMEM((WIN, WIN), F32),
            pltpu.VMEM((WIN, 3 * D), BF16),
            pltpu.VMEM((D, 3 * D), F32),
            pltpu.VMEM((WIN, D), BF16),
        ],
        wins * 5_000_000_000,
        wins * 8_000_000,
    )


def swap(values, axis, size, k):
    return lax.ppermute(values, axis, [(i, i ^ k) for i in range(size)])


def bits_of(size):
    return [1 << i for i in range(size.bit_length() - 1)]


def hop_orders(seq_count):
    high = [k for k in bits_of(seq_count) if k > 1]
    return (high, high[::-1])


def gather_rows(cur, order, seq_count, seq_index):
    blocks, rows, cols = cur.shape
    for k in order:
        got = swap(cur, "seq", seq_count, k)
        odd = (seq_index & k) != 0
        cur = jnp.stack([jnp.where(odd, got, cur), jnp.where(odd, cur, got)], axis=0)
    lead = list(order[::-1])
    count = len(lead)
    axes = [count] + [lead.index(k) for k in sorted(lead, reverse=True)] + [count + 1, count + 2]
    return cur.transpose(axes).reshape(blocks, rows * seq_count, cols)


def gather_split(cur, seq_count, seq_index):
    first, second = hop_orders(seq_count)
    half = cur.shape[0] // 2
    return jnp.concatenate(
        [
            gather_rows(cur[:half], first + [1], seq_count, seq_index),
            gather_rows(cur[half:], second + [1], seq_count, seq_index),
        ],
        axis=0,
    )


def scatter_rows(cur, order, seq_count, seq_index):
    blocks, height, cols = cur.shape
    left = sorted(bits_of(seq_count), reverse=True)
    cur = cur.reshape([blocks] + [2] * len(left) + [height // seq_count, cols])
    for k in order:
        axis = 1 + left.index(k)
        bit = (seq_index // k) % 2
        mine = lax.dynamic_index_in_dim(cur, bit, axis, keepdims=False)
        other = lax.dynamic_index_in_dim(cur, 1 - bit, axis, keepdims=False)
        got = swap(other, "seq", seq_count, k)
        cur = (mine.astype(F32) + got.astype(F32)).astype(BF16)
        left.remove(k)
    return cur


def scatter_split(cur, seq_count, seq_index):
    first, second = hop_orders(seq_count)
    half = cur.shape[0] // 2
    return jnp.concatenate(
        [
            scatter_rows(cur[:half], [1] + first, seq_count, seq_index),
            scatter_rows(cur[half:], [1] + second, seq_count, seq_index),
        ],
        axis=0,
    )


def scatter_parts(cur, parts, dp_count, dp_index):
    owned = cur.shape[0] // len(parts)
    cur = cur.reshape((len(parts), owned) + cur.shape[1:])

    def slab(target):
        at = jnp.clip(target - parts[0], 0, len(parts) - 1)
        return lax.dynamic_index_in_dim(cur, at, 0, keepdims=False)

    total = slab(dp_index).astype(F32)
    for s in range(1, dp_count):
        pairs = [(i, i ^ s) for i in range(dp_count) if (i ^ s) in parts]
        got = lax.ppermute(slab(dp_index ^ s), "dp", pairs)
        total = total + got.astype(F32)
    return total


def gather_parts(own, parts, dp_count, dp_index):
    got = [own]
    for s in range(1, dp_count):
        got.append(
            lax.ppermute(own, "dp", [(i, i ^ s) for i in range(dp_count) if i in parts])
        )
    return jnp.concatenate([lax.select_n(dp_index ^ j, *got) for j in parts], axis=0)


def after(values, *marks):
    return lax.optimization_barrier((values, marks))[0]


def body(
    inputs,
    cotangent,
    lengths,
    weights,
    vectors,
    positions,
    left_stats,
    right_stats,
    left_roots,
    right_roots,
    vector_second,
    position_second,
):
    seq_count = lax.axis_size("seq")
    dp_count = lax.axis_size("dp")
    seq_index = lax.axis_index("seq")
    dp_index = lax.axis_index("dp")
    micro, wins_dev, segment, model_width = inputs.shape
    wins = wins_dev // dp_count
    total_tokens = micro * wins_dev * seq_count * segment * dp_count
    owned, row_part, _ = weights.shape
    qkv_parts = list(range(QKV_BLOCKS // owned))
    rest_parts = list(range(QKV_BLOCKS // owned, dp_count))

    own = weights.astype(BF16)
    qkv_rows = gather_parts(own, qkv_parts, dp_count, dp_index)
    stack_qkv = gather_split(qkv_rows, seq_count, seq_index)
    rest_rows = gather_parts(after(own, qkv_rows), rest_parts, dp_count, dp_index)
    stack_rest = gather_split(rest_rows, seq_count, seq_index)
    roots_full = lax.all_gather(right_roots.astype(BF16), "seq", axis=1, tiled=True)

    vec = vectors.reshape(-1, D)
    bias_qv = jnp.concatenate([vec[0:2], jnp.zeros((6, D), F32)], axis=0)
    vec_pad = jnp.concatenate([vec, jnp.zeros((ROWS_VEC - vec.shape[0], D), F32)], axis=0)

    def exchange(pieces):
        return [pieces[0]] + [swap(pieces[s], "dp", dp_count, s) for s in range(1, dp_count)]

    def send_segments(rows, shift, mark):
        grouped = rows.reshape(dp_count, wins, segment, model_width)
        pieces = []
        for s in range(dp_count):
            piece = lax.dynamic_index_in_dim(grouped, dp_index ^ s, 0, keepdims=False)
            if shift is not None:
                piece = (piece.astype(F32) + shift[None]).astype(BF16)
            pieces.append(piece)
        if mark is not None:
            pieces = after(pieces, mark)
        return exchange(pieces)

    metas = []
    for i in range(micro):
        lens = lax.dynamic_index_in_dim(
            lengths[i].reshape(dp_count, wins), dp_index, 0, keepdims=False
        )
        metas.append(jnp.concatenate([dp_index[None].astype(jnp.int32), lens]))

    xs, cots = [], []
    marks = [qkv_rows, rest_rows]
    for i in range(micro):
        x = send_segments(inputs[i], positions, marks[-2])
        marks.append(x[-1])
        c = send_segments(cotangent[i], None, marks[-2])
        marks.append(c[-1])
        xs.append(x)
        cots.append(c)

    out_got, dx_got = [], []
    dw_rest, dw_qkv = None, None
    vec_grads = jnp.zeros((ROWS_VEC, D), F32)
    for i in range(micro):
        hidden, qkv, attended, lse = call_attention(
            dp_count, segment, metas[i], xs[i], stack_qkv, bias_qv
        )
        results = call_ffn(
            dp_count, segment, total_tokens, metas[i], cots[i], hidden, attended, stack_rest,
            vec_pad, dw_rest,
        )
        outs = results[:dp_count]
        d_mixed, d_o, dw_rest, vg = results[dp_count:]
        out_got.append(exchange(outs))
        results = call_attention_back(
            dp_count, segment, metas[i], stack_qkv, hidden, qkv, d_o, lse, d_mixed, dw_qkv
        )
        dxs = results[:dp_count]
        dw_qkv, db = results[dp_count:]
        dx_got.append(exchange(dxs))
        vec_grads = vec_grads + vg + jnp.concatenate(
            [db[0:2], jnp.zeros((ROWS_VEC - 2, D), F32)], axis=0
        )

    rest_sum = scatter_parts(
        scatter_split(dw_rest, seq_count, seq_index), rest_parts, dp_count, dp_index
    )
    qkv_sum = scatter_parts(
        scatter_split(dw_qkv, seq_count, seq_index), qkv_parts, dp_count, dp_index
    )
    grad_rows = jnp.where(dp_index < len(qkv_parts), qkv_sum, rest_sum)
    grad_low = grad_rows.astype(BF16)
    grad_full = gather_split(grad_low, seq_count, seq_index)

    row_start = seq_index * row_part

    def batched(spec, left, right):
        return jnp.einsum(spec, left, right, preferred_element_type=F32)

    left_new = DECAY * left_stats + (1.0 - DECAY) * batched("bij,bkj->bik", grad_low, grad_full)
    column_part = lax.dynamic_slice_in_dim(grad_full, row_start, row_part, 2)
    right_new = DECAY * right_stats + (1.0 - DECAY) * batched(
        "bki,bkj->bij", column_part, grad_full
    )
    left_applied = batched("bij,bjk->bik", left_roots.astype(BF16), grad_full)
    step_rows = batched("bij,bjk->bik", left_applied.astype(BF16), roots_full)
    weights_new = weights - MATRIX_RATE * step_rows

    sums = vec_grads
    for k in bits_of(seq_count):
        sums = sums + swap(sums, "seq", seq_count, k)
    for k in bits_of(dp_count):
        sums = sums + swap(sums, "dp", dp_count, k)
    vector_grads = sums[: vec.shape[0]].reshape(-1)
    vector_second_new = DECAY * vector_second + (1.0 - DECAY) * vector_grads * vector_grads
    vectors_new = vectors - VECTOR_RATE * vector_grads / (jnp.sqrt(vector_second_new) + ROOT_EPS)

    place_sum = jnp.zeros((segment, model_width), F32)
    layer_rows, input_rows = [], []
    for i in range(micro):
        for got in dx_got[i]:
            place_sum = place_sum + jnp.sum(got.astype(F32), axis=0)
        layer_rows.append(
            jnp.concatenate([lax.select_n(dp_index ^ e, *out_got[i]) for e in range(dp_count)])
        )
        input_rows.append(
            jnp.concatenate(
                [lax.select_n(dp_index ^ e, *dx_got[i]).astype(F32) for e in range(dp_count)]
            )
        )
    for k in bits_of(seq_count):
        low = place_sum.astype(BF16)
        place_sum = low.astype(F32) + swap(low, "seq", seq_count, k).astype(F32)
    position_grads = place_sum
    position_second_new = DECAY * position_second + (1.0 - DECAY) * position_grads * position_grads
    positions_new = positions - VECTOR_RATE * position_grads / (
        jnp.sqrt(position_second_new) + ROOT_EPS
    )
    return (
        jnp.stack(layer_rows, axis=0),
        jnp.stack(input_rows, axis=0),
        grad_rows,
        left_new,
        right_new,
        weights_new,
        vector_grads,
        vector_second_new,
        vectors_new,
        position_grads,
        position_second_new,
        positions_new,
    )


def solution(mesh):
    rows = P(None, "seq", "dp", None)
    blocks = P("dp", "seq", None)
    in_specs = (
        rows, rows, P(None, "seq"), blocks, P(), P("dp", None),
        blocks, blocks, blocks, blocks, P(), P("dp", None),
    )
    out_specs = (
        rows, rows, blocks, blocks, blocks, blocks,
        P(), P(), P(), P("dp", None), P("dp", None), P("dp", None),
    )
    return jax.shard_map(body, mesh=mesh, in_specs=in_specs, out_specs=out_specs, check_vma=False)
```

time: 1020 us -> 460 us (0.45)
  the two profiles are of different devices: /device:TPU:0 before, /device:TPU:17 now
where the time goes in v1:
time: 460 us; the launch traced here: 455 us
  waiting for transfers between devices  142 us (31%)
  Pallas kernels  139 us (30%)
  starting transfers between devices  97.4 us (21%)
  other arithmetic  33.6 us (7%)
  local copies, waits for them, and re-layouts  21 us (5%)
  between operations  15.9 us (3%)
  matrix products  5.63 us (1%)
    pallas_call x6, Pallas kernels, run_kernel(): pl.pallas_call(kernel, grid_spec=pltpu.PrefetchScalarGridSpec(num_scalar_...  139 us
    ppermute x62, waiting for transfers between devices, swap(): return lax.ppermute(values, axis, [(i, i ^ k) for i in range(size)])  128 us
    ppermute x62, starting transfers between devices, swap(): return lax.ppermute(values, axis, [(i, i ^ k) for i in range(size)])  70.6 us
    ppermute x6, starting transfers between devices, gather_parts(): lax.ppermute(own, 'dp', [(i, i ^ s) for i in range(dp_count) if i in parts])  15.5 us
    ppermute x6, starting transfers between devices, scatter_parts(): got = lax.ppermute(slab(dp_index ^ s), 'dp', pairs)  11.3 us
  transfers between devices with their start and end apart: 75, of which 30 were waited for; matrix products, arithmetic and copies ran while one was open for 12% of the time, Pallas kernels for 31%

profile of v1, /device:TPU:17, one launch (start us, length us, event | category | flops | bytes accessed | tf_op | source)
XLA Modules:
  0.0 454.8 jit_solution(3457847521268567826)
XLA Ops:
  27.1 7.6 %collective-permute-start.15 = (bf16[12,32,256]{2,1,0:T(8,128)(2,1)}, bf16[12,32,256]{2,1,0:T(8,128)(2,1)S(1)}, u32[]{:S(2)}, u32[]{:S(2)}) collective-permute-start(bf16[12,32,256]{2,1,0:T(8,128)(2,1)} %convert_element_type.330), channel_id=1, source_target_pairs={{1,0},{2,3},{3,2},{5,4},{6,7},{7,6},{9,8},{10,11},{11,10},{13,12},... | collective-permute-start | bytes 589832 | tf_op jit(solution)/shard_map/ppermute | solution.py:579
  43.3 9.1 %collective-permute-done.17 = bf16[12,32,256]{2,1,0:T(8,128)(2,1)S(1)} collective-permute-done((bf16[12,32,256]{2,1,0:T(8,128)(2,1)}, bf16[12,32,256]{2,1,0:T(8,128)(2,1)S(1)}, u32[]{:S(2)}, u32[]{:S(2)}) %collective-permute-start.17) | collective-permute-done | bytes 196640 | tf_op jit(solution)/shard_map/ppermute | solution.py:579
  53.7 20.9 %collective-permute-done.8.refs_3_ = bf16[2,128,512]{2,1,0:T(8,128)(2,1)S(1)} collective-permute-done((bf16[2,128,512]{2,1,0:T(8,128)(2,1)S(1)}, bf16[2,128,512]{2,1,0:T(8,128)(2,1)S(1)}, u32[]{:S(2)}, u32[]{:S(2)}) %collective-permute-start.8) | collective-permute-done | bytes 262176 | tf_op jit(solution)/shard_map/ppermute | solution.py:496
  75.6 5.6 %collective-permute-done.18 = bf16[18,32,256]{2,1,0:T(8,128)(2,1)S(1)} collective-permute-done((bf16[18,32,256]{2,1,0:T(8,128)(2,1)S(1)}, bf16[18,32,256]{2,1,0:T(8,128)(2,1)S(1)}, u32[]{:S(2)}, u32[]{:S(2)}) %collective-permute-start.18) | collective-permute-done | bytes 294944 | tf_op jit(solution)/shard_map/ppermute | solution.py:496
  88.5 11.4 %collective-permute-done.19 = bf16[2,18,32,256]{3,2,1,0:T(8,128)(2,1)S(1)} collective-permute-done((bf16[2,18,32,256]{3,2,1,0:T(8,128)(2,1)S(1)}, bf16[2,18,32,256]{3,2,1,0:T(8,128)(2,1)S(1)}, u32[]{:S(2)}, u32[]{:S(2)}) %collective-permute-start.19) | collective-permute-done | bytes 589856 | tf_op jit(solution)/shard_map/ppermute | solution.py:496
  104.7 15.2 %shard_map.211 = (bf16[2,512,512]{2,1,0:T(8,128)(2,1)}, bf16[2,512,1536]{2,1,0:T(8,128)(2,1)}, bf16[2,512,512]{2,1,0:T(8,128)(2,1)}, f32[2,8,512]{2,1,0:T(8,128)}) custom-call(s32[3]{0:T(128)} %pad_add_fusion.1.meta, bf16[2,128,512]{2,1,0:T(8,128)(2,1)} %get-tuple-element.69.refs_0_, bf16[2,128,512]{2,1,0:T(8,128)(2,1)} %collective-permute-done.6.refs_1_, ...), custom_call_target="tpu_custom_call" | custom-call | flops 8000000000 | bytes 8000000 | tf_op jit(solution)/shard_map/pallas_call | solution.py:365
  125.8 15.1 %shard_map.213 = (bf16[2,512,512]{2,1,0:T(8,128)(2,1)}, bf16[2,512,1536]{2,1,0:T(8,128)(2,1)}, bf16[2,512,512]{2,1,0:T(8,128)(2,1)}, f32[2,8,512]{2,1,0:T(8,128)}) custom-call(s32[3]{0:T(128)} %pad_add_fusion.2.meta, bf16[2,128,512]{2,1,0:T(8,128)(2,1)} %get-tuple-element.84.refs_0_, bf16[2,128,512]{2,1,0:T(8,128)(2,1)} %collective-permute-done.30.refs_1_, ...), custom_call_target="tpu_custom_call" | custom-call | flops 8000000000 | bytes 8000000 | tf_op jit(solution)/shard_map/pallas_call | solution.py:365
  147.5 31.0 %shard_map.212 = (bf16[2,128,512]{2,1,0:T(8,128)(2,1)}, bf16[2,128,512]{2,1,0:T(8,128)(2,1)}, bf16[2,128,512]{2,1,0:T(8,128)(2,1)}, bf16[2,128,512]{2,1,0:T(8,12...) custom-call(s32[3]{0:T(128)} %pad_add_fusion.1.meta, ...), custom_call_target="tpu_custom_call" | custom-call | flops 16000000000 | bytes 24000000 | tf_op jit(solution)/shard_map/pallas_call | solution.py:365
  178.5 22.1 %shard_map.215 = (bf16[2,128,512]{2,1,0:T(8,128)(2,1)}, bf16[2,128,512]{2,1,0:T(8,128)(2,1)}, bf16[2,128,512]{2,1,0:T(8,128)(2,1)}, bf16[2,128,512]{2,1,0:T(8,12...) custom-call(s32[3]{0:T(128)} %pad_add_fusion.1.meta, bf16[12,256,256]{2,1,0:T(8,128)(2,1)} %pad_maximum_fusion.3.refs_4_.refs_0_, ...), custom_call_target="tpu_custom_call" | custom-call | flops 10000000000 | bytes 16000000 | tf_op jit(solution)/shard_map/pallas_call | solution.py:365
  200.6 32.4 %shard_map.214 = (bf16[2,128,512]{2,1,0:T(8,128)(2,1)}, bf16[2,128,512]{2,1,0:T(8,128)(2,1)}, bf16[2,128,512]{2,1,0:T(8,128)(2,1)}, bf16[2,128,512]{2,1,0:T(8,12...) custom-call(s32[3]{0:T(128)} %pad_add_fusion.2.meta, ...), custom_call_target="tpu_custom_call" | custom-call | flops 16000000000 | bytes 24000000 | tf_op jit(solution)/shard_map/pallas_call | solution.py:365
  233.1 23.1 %shard_map.216 = (bf16[2,128,512]{2,1,0:T(8,128)(2,1)}, bf16[2,128,512]{2,1,0:T(8,128)(2,1)}, bf16[2,128,512]{2,1,0:T(8,128)(2,1)}, bf16[2,128,512]{2,1,0:T(8,12...) custom-call(s32[3]{0:T(128)} %pad_add_fusion.2.meta, bf16[12,256,256]{2,1,0:T(8,128)(2,1)} %pad_maximum_fusion.3.refs_4_.refs_0_, ...), custom_call_target="tpu_custom_call" | custom-call | flops 10000000000 | bytes 16000000 | tf_op jit(solution)/shard_map/pallas_call | solution.py:365
  256.3 3.0 collective-permute-start.40
  275.6 5.7 %collective-permute-done.69 = f32[16,512]{1,0:T(8,128)S(1)} collective-permute-done((f32[16,512]{1,0:T(8,128)S(1)}, f32[16,512]{1,0:T(8,128)S(1)}, u32[]{:S(2)}, u32[]{:S(2)}) %collective-permute-start.69) | collective-permute-done | bytes 32800 | tf_op jit(solution)/shard_map/ppermute | solution.py:496
  284.7 16.7 %collective-permute-done.70 = f32[16,512]{1,0:T(8,128)S(1)} collective-permute-done((f32[16,512]{1,0:T(8,128)S(1)}, f32[16,512]{1,0:T(8,128)S(1)}, u32[]{:S(2)}, u32[]{:S(2)}) %collective-permute-start.70) | collective-permute-done | bytes 32800 | tf_op jit(solution)/shard_map/ppermute | solution.py:496
  301.3 3.8 collective-permute-start.36
  320.6 15.9 %collective-permute-done.26 = bf16[2,128,512]{2,1,0:T(8,128)(2,1)S(1)} collective-permute-done((bf16[2,128,512]{2,1,0:T(8,128)(2,1)}, bf16[2,128,512]{2,1,0:T(8,128)(2,1)S(1)}, u32[]{:S(2)}, u32[]{:S(2)}) %collective-permute-start.26) | collective-permute-done | bytes 262176 | tf_op jit(solution)/shard_map/ppermute | solution.py:496
  338.0 9.2 %collective-permute-done.34 = bf16[2,128,512]{2,1,0:T(8,128)(2,1)S(1)} collective-permute-done((bf16[2,128,512]{2,1,0:T(8,128)(2,1)S(1)}, bf16[2,128,512]{2,1,0:T(8,128)(2,1)S(1)}, u32[]{:S(2)}, u32[]{:S(2)}) %collective-permute-start.34) | collective-permute-done | bytes 262176 | tf_op jit(solution)/shard_map/ppermute | solution.py:496
  347.2 6.7 %collective-permute-start.42 = (bf16[6,2,2,32,256]{4,3,0,1,2:T(8,128)(2,1)S(1)}, bf16[6,2,2,32,256]{4,3,0,1,2:T(8,128)(2,1)S(1)}, u32[]{:S(2)}, u32[]{:S(2)}) collective-permute-start(bf16[6,2,2,32,256]{4,3,0,1,2:T(8,128)(2,1)S(1)} %bitcast.256), channel_id=1, source_target_pairs={{0,4},{4,0},{8,12},{12,8},{16,20},{20,16},{24,28},{28,24},{1,5},{5... | collective-permute-start | bytes 1179656 | tf_op jit(solution)/shard_map/ppermute | solution.py:496
  367.9 5.6 %collective-permute-done.43 = bf16[6,2,32,256]{3,2,0,1:T(8,128)(2,1)S(1)} collective-permute-done((bf16[6,2,32,256]{3,2,0,1:T(8,128)(2,1)S(1)}, bf16[6,2,32,256]{3,2,0,1:T(8,128)(2,1)S(1)}, u32[]{:S(2)}, u32[]{:S(2)}) %collective-permute-start.43) | collective-permute-done | bytes 196640 | tf_op jit(solution)/shard_map/ppermute | solution.py:496
  379.1 11.5 %collective-permute-done.52 = bf16[18,2,32,256]{3,2,0,1:T(8,128)(2,1)S(1)} collective-permute-done((bf16[18,2,32,256]{3,2,0,1:T(8,128)(2,1)S(1)}, bf16[18,2,32,256]{3,2,0,1:T(8,128)(2,1)S(1)}, u32[]{:S(2)}, u32[]{:S(2)}) %collective-permute-start.52) | collective-permute-done | bytes 589856 | tf_op jit(solution)/shard_map/ppermute | solution.py:496
  401.3 5.5 %collective-permute-start.59 = (bf16[12,32,256]{2,1,0:T(8,128)(2,1)S(1)}, bf16[12,32,256]{2,1,0:T(8,128)(2,1)S(1)}, u32[]{:S(2)}, u32[]{:S(2)}) collective-permute-start(bf16[12,32,256]{2,1,0:T(8,128)(2,1)S(1)} %get-tuple-element.193), channel_id=1, source_target_pairs={{0,3},{1,2},{2,1},{4,7},{5,6},{6,5},{8,11},{9,10},{10,9},{12,15},{... | collective-permute-start | bytes 589832 | tf_op jit(solution)/shard_map/ppermute | solution.py:570
  409.1 5.3 %collective-permute-start.71 = (bf16[128,512]{1,0:T(8,128)(2,1)S(1)}, bf16[128,512]{1,0:T(8,128)(2,1)S(1)}, u32[]{:S(2)}, u32[]{:S(2)}) collective-permute-start(bf16[128,512]{1,0:T(8,128)(2,1)S(1)} %add_convert_fusion.2), channel_id=1, source_target_pairs={{0,4},{4,0},{8,12},{12,8},{16,20},{20,16},{24,28},{28,24},{1,5},{5... | collective-permute-start | bytes 393224 | tf_op jit(solution)/shard_map/ppermute | solution.py:496
  414.3 5.6 %collective-permute-done.59 = bf16[12,32,256]{2,1,0:T(8,128)(2,1)S(1)} collective-permute-done((bf16[12,32,256]{2,1,0:T(8,128)(2,1)S(1)}, bf16[12,32,256]{2,1,0:T(8,128)(2,1)S(1)}, u32[]{:S(2)}, u32[]{:S(2)}) %collective-permute-start.59) | collective-permute-done | bytes 196640 | tf_op jit(solution)/shard_map/ppermute | solution.py:570
  431.7 5.5 %collective-permute-start.62 = (bf16[2,2,6,32,256]{4,3,2,1,0:T(8,128)(2,1)S(1)}, bf16[2,2,6,32,256]{4,3,2,1,0:T(8,128)(2,1)S(1)}, u32[]{:S(2)}, u32[]{:S(2)}) collective-permute-start(bf16[2,2,6,32,256]{4,3,2,1,0:T(8,128)(2,1)S(1)} %pad_maximum_fusion.15), channel_id=1, source_target_pairs={{0,4},{4,0},{8,12},{12,8},{16,20},{20,16},{24,28},{28,24},{1,5},{5... | collective-permute-start | bytes 1179656 | tf_op jit(solution)/shard_map/ppermute | solution.py:496
  (334 shorter events, 145.6 us)
Async XLA Ops:
  7.2 437.5 %all-gather.2.cloned.1.call-start = ((), (), s32[]{:S(2)}) async-start(), calls=%async_computation | async-start | bytes 1769472 | tf_op jit(solution)/shard_map/all_gather | solution.py:618
  15.7 21.4 %collective-permute-start.2 = (bf16[2,128,512]{2,1,0:T(8,128)(2,1)}, bf16[2,128,512]{2,1,0:T(8,128)(2,1)}, u32[]{:S(2)}, u32[]{:S(2)}) collective-permute-start(bf16[2,128,512]{2,1,0:T(8,128)(2,1)} %get-tuple-element.68), channel_id=1, source_target_pairs={{0,3},{1,2},{2,1},{3,0},{4,7},{5,6},{6,5},{7,4},{8,11},{9,10},{10,... | collective-permute-start | bytes 786440 | tf_op jit(solution)/shard_map/ppermute | solution.py:496
  39.8 63.3 %collective-permute-start.6 = (bf16[2,128,512]{2,1,0:T(8,128)(2,1)S(1)}, bf16[2,128,512]{2,1,0:T(8,128)(2,1)}, u32[]{:S(2)}, u32[]{:S(2)}) collective-permute-start(bf16[2,128,512]{2,1,0:T(8,128)(2,1)S(1)} %get-tuple-element.70), channel_id=1, source_target_pairs={{0,1},{1,0},{2,3},{3,2},{4,5},{5,4},{6,7},{7,6},{8,9},{9,8},{10,11... | collective-permute-start | bytes 786440 | tf_op jit(solution)/shard_map/ppermute | solution.py:496
  39.9 64.8 %collective-permute-start.7 = (bf16[2,128,512]{2,1,0:T(8,128)(2,1)S(1)}, bf16[2,128,512]{2,1,0:T(8,128)(2,1)}, u32[]{:S(2)}, u32[]{:S(2)}) collective-permute-start(bf16[2,128,512]{2,1,0:T(8,128)(2,1)S(1)} %get-tuple-element.71), channel_id=1, source_target_pairs={{0,2},{1,3},{2,0},{3,1},{4,6},{5,7},{6,4},{7,5},{8,10},{9,11},{10,... | collective-permute-start | bytes 786440 | tf_op jit(solution)/shard_map/ppermute | solution.py:496
  41.9 32.7 %collective-permute-start.8 = (bf16[2,128,512]{2,1,0:T(8,128)(2,1)S(1)}, bf16[2,128,512]{2,1,0:T(8,128)(2,1)S(1)}, u32[]{:S(2)}, u32[]{:S(2)}) collective-permute-start(bf16[2,128,512]{2,1,0:T(8,128)(2,1)S(1)} %get-tuple-element.72), channel_id=1, source_target_pairs={{0,3},{1,2},{2,1},{3,0},{4,7},{5,6},{6,5},{7,4},{8,11},{9,10},{10,... | collective-permute-start | bytes 786440 | tf_op jit(solution)/shard_map/ppermute | solution.py:496
  42.7 32.1 %collective-permute-start.10 = (bf16[2,6,32,256]{3,2,1,0:T(8,128)(2,1)S(1)}, bf16[2,6,32,256]{3,2,1,0:T(8,128)(2,1)S(1)}, u32[]{:S(2)}, u32[]{:S(2)}) collective-permute-start(bf16[2,6,32,256]{3,2,1,0:T(8,128)(2,1)S(1)} %pad_maximum_fusion.19), channel_id=1, source_target_pairs={{0,16},{4,20},{8,24},{12,28},{16,0},{20,4},{24,8},{28,12},{1,17},{... | collective-permute-start | bytes 589832 | tf_op jit(solution)/shard_map/ppermute | solution.py:496
  52.3 23.1 %collective-permute-start.13 = (bf16[2,6,32,256]{3,2,1,0:T(8,128)(2,1)S(1)}, bf16[2,6,32,256]{3,2,1,0:T(8,128)(2,1)S(1)}, u32[]{:S(2)}, u32[]{:S(2)}) collective-permute-start(bf16[2,6,32,256]{3,2,1,0:T(8,128)(2,1)S(1)} %pad_maximum_fusion.20), channel_id=1, source_target_pairs={{0,8},{4,12},{8,0},{12,4},{16,24},{20,28},{24,16},{28,20},{1,9},{5... | collective-permute-start | bytes 589832 | tf_op jit(solution)/shard_map/ppermute | solution.py:496
  75.5 44.5 %collective-permute-start.30 = (bf16[2,128,512]{2,1,0:T(8,128)(2,1)}, bf16[2,128,512]{2,1,0:T(8,128)(2,1)}, u32[]{:S(2)}, u32[]{:S(2)}) collective-permute-start(bf16[2,128,512]{2,1,0:T(8,128)(2,1)} %get-tuple-element.85), channel_id=1, source_target_pairs={{0,1},{1,0},{2,3},{3,2},{4,5},{5,4},{6,7},{7,6},{8,9},{9,8},{10,11... | collective-permute-start | bytes 786440 | tf_op jit(solution)/shard_map/ppermute | solution.py:496
  99.9 21.3 %collective-permute-start.31 = (bf16[2,128,512]{2,1,0:T(8,128)(2,1)}, bf16[2,128,512]{2,1,0:T(8,128)(2,1)}, u32[]{:S(2)}, u32[]{:S(2)}) collective-permute-start(bf16[2,128,512]{2,1,0:T(8,128)(2,1)} %get-tuple-element.86), channel_id=1, source_target_pairs={{0,2},{1,3},{2,0},{3,1},{4,6},{5,7},{6,4},{7,5},{8,10},{9,11},{10,... | collective-permute-start | bytes 786440 | tf_op jit(solution)/shard_map/ppermute | solution.py:496
  100.6 25.3 %collective-permute-start.32 = (bf16[2,128,512]{2,1,0:T(8,128)(2,1)}, bf16[2,128,512]{2,1,0:T(8,128)(2,1)}, u32[]{:S(2)}, u32[]{:S(2)}) collective-permute-start(bf16[2,128,512]{2,1,0:T(8,128)(2,1)} %get-tuple-element.87), channel_id=1, source_target_pairs={{0,3},{1,2},{2,1},{3,0},{4,7},{5,6},{6,5},{7,4},{8,11},{9,10},{10,... | collective-permute-start | bytes 786440 | tf_op jit(solution)/shard_map/ppermute | solution.py:496
  103.1 37.8 %collective-permute-start.20 = (bf16[2,2,18,32,256]{4,3,2,1,0:T(8,128)(2,1)S(1)}, bf16[2,2,18,32,256]{4,3,2,1,0:T(8,128)(2,1)S(1)}, u32[]{:S(2)}, u32[]{:S(2)}) collective-permute-start(bf16[2,2,18,32,256]{4,3,2,1,0:T(8,128)(2,1)S(1)} %pad_maximum_fusion.4), channel_id=1, source_target_pairs={{0,4},{4,0},{8,12},{12,8},{16,20},{20,16},{24,28},{28,24},{1,5},{5... | collective-permute-start | bytes 3538952 | tf_op jit(solution)/shard_map/ppermute | solution.py:496
  104.7 36.8 %collective-permute-start.23 = (bf16[2,2,18,32,256]{4,3,2,1,0:T(8,128)(2,1)S(1)}, bf16[2,2,18,32,256]{4,3,2,1,0:T(8,128)(2,1)S(1)}, u32[]{:S(2)}, u32[]{:S(2)}) collective-permute-start(bf16[2,2,18,32,256]{4,3,2,1,0:T(8,128)(2,1)S(1)} %pad_maximum_fusion.5), channel_id=1, source_target_pairs={{0,4},{4,0},{8,12},{12,8},{16,20},{20,16},{24,28},{28,24},{1,5},{5... | collective-permute-start | bytes 3538952 | tf_op jit(solution)/shard_map/ppermute | solution.py:496
  120.0 27.5 %collective-permute-start = (bf16[2,128,512]{2,1,0:T(8,128)(2,1)S(1)}, bf16[2,128,512]{2,1,0:T(8,128)(2,1)}, u32[]{:S(2)}, u32[]{:S(2)}) collective-permute-start(bf16[2,128,512]{2,1,0:T(8,128)(2,1)S(1)} %copy-done.19), channel_id=1, source_target_pairs={{0,1},{1,0},{2,3},{3,2},{4,5},{5,4},{6,7},{7,6},{8,9},{9,8},{10,11... | collective-permute-start | bytes 786440 | tf_op jit(solution)/shard_map/ppermute | solution.py:496
  121.2 26.3 %collective-permute-start.1 = (bf16[2,128,512]{2,1,0:T(8,128)(2,1)S(1)}, bf16[2,128,512]{2,1,0:T(8,128)(2,1)}, u32[]{:S(2)}, u32[]{:S(2)}) collective-permute-start(bf16[2,128,512]{2,1,0:T(8,128)(2,1)S(1)} %copy-done.18), channel_id=1, source_target_pairs={{0,2},{1,3},{2,0},{3,1},{4,6},{5,7},{6,4},{7,5},{8,10},{9,11},{10,... | collective-permute-start | bytes 786440 | tf_op jit(solution)/shard_map/ppermute | solution.py:496
  125.8 74.8 %collective-permute-start.27 = (bf16[2,128,512]{2,1,0:T(8,128)(2,1)}, bf16[2,128,512]{2,1,0:T(8,128)(2,1)}, u32[]{:S(2)}, u32[]{:S(2)}) collective-permute-start(bf16[2,128,512]{2,1,0:T(8,128)(2,1)} %get-tuple-element.81), channel_id=1, source_target_pairs={{0,1},{1,0},{2,3},{3,2},{4,5},{5,4},{6,7},{7,6},{8,9},{9,8},{10,11... | collective-permute-start | bytes 786440 | tf_op jit(solution)/shard_map/ppermute | solution.py:496
  140.9 59.7 %collective-permute-start.28 = (bf16[2,128,512]{2,1,0:T(8,128)(2,1)S(1)}, bf16[2,128,512]{2,1,0:T(8,128)(2,1)}, u32[]{:S(2)}, u32[]{:S(2)}) collective-permute-start(bf16[2,128,512]{2,1,0:T(8,128)(2,1)S(1)} %get-tuple-element.82), channel_id=1, source_target_pairs={{0,2},{1,3},{2,0},{3,1},{4,6},{5,7},{6,4},{7,5},{8,10},{9,11},{10,... | collective-permute-start | bytes 786440 | tf_op jit(solution)/shard_map/ppermute | solution.py:496
  141.4 59.2 %collective-permute-start.29 = (bf16[2,128,512]{2,1,0:T(8,128)(2,1)S(1)}, bf16[2,128,512]{2,1,0:T(8,128)(2,1)}, u32[]{:S(2)}, u32[]{:S(2)}) collective-permute-start(bf16[2,128,512]{2,1,0:T(8,128)(2,1)S(1)} %get-tuple-element.83), channel_id=1, source_target_pairs={{0,3},{1,2},{2,1},{3,0},{4,7},{5,6},{6,5},{7,4},{8,11},{9,10},{10,... | collective-permute-start | bytes 786440 | tf_op jit(solution)/shard_map/ppermute | solution.py:496
  256.2 103.1 %collective-permute-start.41 = (bf16[2,128,512]{2,1,0:T(8,128)(2,1)}, bf16[2,128,512]{2,1,0:T(8,128)(2,1)}, u32[]{:S(2)}, u32[]{:S(2)}) collective-permute-start(bf16[2,128,512]{2,1,0:T(8,128)(2,1)} %get-tuple-element.111), channel_id=1, source_target_pairs={{0,3},{1,2},{2,1},{3,0},{4,7},{5,6},{6,5},{7,4},{8,11},{9,10},{10,... | collective-permute-start | bytes 786440 | tf_op jit(solution)/shard_map/ppermute | solution.py:496
  256.3 104.4 %collective-permute-start.40 = (bf16[2,128,512]{2,1,0:T(8,128)(2,1)}, bf16[2,128,512]{2,1,0:T(8,128)(2,1)}, u32[]{:S(2)}, u32[]{:S(2)}) collective-permute-start(bf16[2,128,512]{2,1,0:T(8,128)(2,1)} %get-tuple-element.110), channel_id=1, source_target_pairs={{0,2},{1,3},{2,0},{3,1},{4,6},{5,7},{6,4},{7,5},{8,10},{9,11},{10,... | collective-permute-start | bytes 786440 | tf_op jit(solution)/shard_map/ppermute | solution.py:496
  259.2 49.3 %collective-permute-start.38 = (bf16[2,128,512]{2,1,0:T(8,128)(2,1)}, bf16[2,128,512]{2,1,0:T(8,128)(2,1)}, u32[]{:S(2)}, u32[]{:S(2)}) collective-permute-start(bf16[2,128,512]{2,1,0:T(8,128)(2,1)} %get-tuple-element.102), channel_id=1, source_target_pairs={{0,3},{1,2},{2,1},{3,0},{4,7},{5,6},{6,5},{7,4},{8,11},{9,10},{10,... | collective-permute-start | bytes 786440 | tf_op jit(solution)/shard_map/ppermute | solution.py:496
  259.6 49.9 %collective-permute-start.37 = (bf16[2,128,512]{2,1,0:T(8,128)(2,1)}, bf16[2,128,512]{2,1,0:T(8,128)(2,1)}, u32[]{:S(2)}, u32[]{:S(2)}) collective-permute-start(bf16[2,128,512]{2,1,0:T(8,128)(2,1)} %get-tuple-element.101), channel_id=1, source_target_pairs={{0,2},{1,3},{2,0},{3,1},{4,6},{5,7},{6,4},{7,5},{8,10},{9,11},{10,... | collective-permute-start | bytes 786440 | tf_op jit(solution)/shard_map/ppermute | solution.py:496
  310.5 26.0 %collective-permute-start.26 = (bf16[2,128,512]{2,1,0:T(8,128)(2,1)}, bf16[2,128,512]{2,1,0:T(8,128)(2,1)S(1)}, u32[]{:S(2)}, u32[]{:S(2)}) collective-permute-start(bf16[2,128,512]{2,1,0:T(8,128)(2,1)} %get-tuple-element.79), channel_id=1, source_target_pairs={{0,3},{1,2},{2,1},{3,0},{4,7},{5,6},{6,5},{7,4},{8,11},{9,10},{10,... | collective-permute-start | bytes 786440 | tf_op jit(solution)/shard_map/ppermute | solution.py:496
  320.6 26.6 %collective-permute-start.34 = (bf16[2,128,512]{2,1,0:T(8,128)(2,1)S(1)}, bf16[2,128,512]{2,1,0:T(8,128)(2,1)S(1)}, u32[]{:S(2)}, u32[]{:S(2)}) collective-permute-start(bf16[2,128,512]{2,1,0:T(8,128)(2,1)S(1)} %copy-done.31), channel_id=1, source_target_pairs={{0,2},{1,3},{2,0},{3,1},{4,6},{5,7},{6,4},{7,5},{8,10},{9,11},{10,... | collective-permute-start | bytes 786440 | tf_op jit(solution)/shard_map/ppermute | solution.py:496
  338.0 25.8 %collective-permute-start.39 = (bf16[2,128,512]{2,1,0:T(8,128)(2,1)S(1)}, bf16[2,128,512]{2,1,0:T(8,128)(2,1)S(1)}, u32[]{:S(2)}, u32[]{:S(2)}) collective-permute-start(bf16[2,128,512]{2,1,0:T(8,128)(2,1)S(1)} %copy-done.29), channel_id=1, source_target_pairs={{0,1},{1,0},{2,3},{3,2},{4,5},{5,4},{6,7},{7,6},{8,9},{9,8},{10,11... | collective-permute-start | bytes 786440 | tf_op jit(solution)/shard_map/ppermute | solution.py:496
  (86 other events, 871.6 us)
Sparse Core Ops, SparseCore 0:
  16.7 34.9 all-gather.1
